TPU v7x, 32 devices: a whole 2x2x4 slice. The times are simulated.
32 devices in a mesh: grp: 2 (over y), az: 4 (over x, core), ax: 4 (over z).
Axes of the slice: x: 2, y: 2, z: 4, core: 2. Of those that a mesh axis runs over, the one named last changes fastest.
Arguments:
- populations: float32 [2, 27, 2, 128, 512], P('grp', None, None, 'az', 'ax'), may hold values from 0.4 to 1.6
- relax_rates: float32 [2, 27], replicated, may hold values from 1 to 1.7
- tile_offsets: int32 [4, 4], P('ax'), may hold values from 0 to 3, each once within a row
Outputs:
- populations_next: float32 [2, 27, 2, 128, 512], P('grp', None, None, 'az', 'ax')
Inputs may be any that keep to these rules, and one draw needn't show every extreme that they name: `tile_offsets`: each row is a permutation of the 4 block offsets.
All inputs are finite; a program needn't handle non-finite values.
Results may differ from a plain program's by a relative error of at most 0.0003.
Values sent between devices are 32-bit elements; how exact they have to be, the bound alone decides.
A program may use at most 64 MiB of HBM per device.

v0:
```python
import jax
import jax.numpy as jnp
from jax import lax
from jax.sharding import PartitionSpec as P

exact_mode = lax.Precision.HIGHEST


def padded_2(x, sides, width):
    for axis, dim in sides:
        size, length = (lax.axis_size(axis), x.shape[dim])
        up = [(i, (i + 1) % size) for i in range(size)]
        down = [(j, i) for i, j in up]
        last = lax.slice_in_dim(x, length - width, length, axis=dim)
        first = lax.slice_in_dim(x, 0, width, axis=dim)
        before = lax.ppermute(last, axis, up)
        after = lax.ppermute(first, axis, down)
        x = jnp.concatenate([before, x, after], axis=dim)
    return x


def single_weight(value):
    return 2.0 / 3.0 if value == 0 else 1.0 / 6.0


def lattice_tables():
    speeds = [
        (radial, beside_all, along)
        for radial in (-1, 0, 1)
        for beside_all in (-1, 0, 1)
        for along in (-1, 0, 1)
    ]
    weights = [
        single_weight(vector[0]) * single_weight(vector[1]) * single_weight(vector[2])
        for vector in speeds
    ]
    powers = [
        (first, second, third) for first in range(3) for second in range(3) for third in range(3)
    ]
    moments = [
        [
            float(vector[0] ** power[0] * vector[1] ** power[1] * vector[2] ** power[2])
            for vector in speeds
        ]
        for power in powers
    ]
    inverse_one = {-1: (0.0, -0.5, 0.5), 0: (1.0, 0.0, -1.0), 1: (0.0, 0.5, 0.5)}
    inverse = [
        [
            inverse_one[vector[0]][power[0]]
            * inverse_one[vector[1]][power[1]]
            * inverse_one[vector[2]][power[2]]
            for power in powers
        ]
        for vector in speeds
    ]
    return (speeds, weights, moments, inverse)


def operators(relax_rates):
    speeds, weights, moments, inverse = lattice_tables()
    keeping = [0.0 if index in (0, 1, 3, 9) else 1.0 for index in range(27)]
    left_table = jnp.asarray(
        [[inverse[row][col] / weights[row] for col in range(27)] for row in range(27)],
        dtype=jnp.float32,
    )
    right_table = jnp.asarray(
        [[moments[row][col] * weights[col] for col in range(27)] for row in range(27)],
        dtype=jnp.float32,
    )
    scaled = relax_rates * jnp.asarray(keeping, dtype=jnp.float32)
    return jnp.einsum("im,gm,mj->gij", left_table, scaled, right_table, precision=exact_mode)


def equilibrium(state):
    speeds, weights, moments, inverse = lattice_tables()
    weight_table = jnp.asarray(weights, dtype=jnp.float32)
    drift_table = jnp.asarray(
        [[float(speeds[row][col]) * weights[row] for col in range(3)] for row in range(27)],
        dtype=jnp.float32,
    )
    speed_table = jnp.asarray(
        [[float(speeds[row][col]) for col in range(3)] for row in range(27)], dtype=jnp.float32
    )
    density = jnp.einsum("i,i...->...", weight_table, state, precision=exact_mode)
    flow = jnp.einsum("ik,i...->k...", drift_table, state, precision=exact_mode) / density
    project = jnp.einsum("ik,k...->i...", speed_table, flow, precision=exact_mode)
    square = jnp.sum(flow * flow, axis=0)
    return density * (1.0 + 3.0 * project + 4.5 * project * project - 1.5 * square)


def relax(state, collision_matrix):
    return state - jnp.einsum(
        "ij,j...->i...", collision_matrix, state - equilibrium(state), precision=exact_mode
    )


def stream(padded, low_ghost, high_ghost, beside_all, axial):
    outgoing = []
    for index in range(27):
        radial_step = index // 9 - 1
        around_step = index // 3 % 3 - 1
        along_step = index % 3 - 1
        moved = padded[
            index,
            :,
            1 - around_step : 1 - around_step + beside_all,
            1 - along_step : 1 - along_step + axial,
        ]
        if radial_step == 1:
            moved = jnp.concatenate([low_ghost[index - 18][None], moved[:-1]], axis=0)
        elif radial_step == -1:
            moved = jnp.concatenate([moved[1:], high_ghost[index][None]], axis=0)
        outgoing.append(moved)
    return jnp.stack(outgoing)


def bounced(post):
    return jnp.stack([post[26 - index, -1] for index in range(9)])


def mirrored(padded, beside_all, axial):
    rows = []
    for index in range(18, 27):
        around_step = index // 3 % 3 - 1
        along_step = index % 3 - 1
        rows.append(
            padded[
                index - 18,
                0,
                1 - around_step : 1 - around_step + beside_all,
                1 - along_step : 1 - along_step + axial,
            ]
        )
    return jnp.stack(rows)


def local(populations, relax_rates, tile_offsets):
    state = populations[0]
    group = lax.axis_index("grp")
    place = lax.axis_index("az")
    count = lax.axis_size("az")
    beside_all = state.shape[2]
    axial = state.shape[3]
    slots = beside_all // count
    annulus = group == 0
    matrices = operators(relax_rates)
    own_matrix = matrices[group]
    fine_matrix = matrices[0]
    rate_fine = relax_rates[0, 12]
    rate_core = relax_rates[1, 12]

    def own_collision(block):
        return relax(block, own_matrix)

    def second_collision(block):
        return relax(block, fine_matrix)

    def advance(block, collide):
        post = collide(block)
        padded = padded_2(post, (("az", 2), ("ax", 3)), 1)
        return (post, padded)

    post_first, padded_first = advance(state, own_collision)
    face_rows = jnp.where(annulus, post_first[:, 0], post_first[:, -1])
    face_balance = equilibrium(face_rows)
    to_core = face_balance[0:9] + 2.0 * rate_fine / rate_core * (face_rows[0:9] - face_balance[0:9])
    to_annulus = face_balance[18:27] + rate_core / (2.0 * rate_fine) * (
        face_rows[18:27] - face_balance[18:27]
    )
    outward = jnp.where(annulus, to_core, to_annulus).reshape(9, count, slots, axial)
    direction = 1 - 2 * group
    partner = jnp.remainder(place + direction * tile_offsets[0], count)
    selector = (jnp.arange(count, dtype=jnp.int32)[:, None] == partner[None, :]).astype(jnp.float32)
    outbound = jnp.einsum("dg,igsx->disx", selector, outward, precision=exact_mode)
    blank = jnp.zeros_like(outbound)
    stacked = jnp.where(
        annulus,
        jnp.concatenate([blank, outbound], axis=0),
        jnp.concatenate([outbound, blank], axis=0),
    )
    mixed = lax.all_to_all(stacked, ("grp", "az"), split_axis=0, concat_axis=0, tiled=True)
    received = lax.dynamic_slice_in_dim(mixed, (1 - group) * count, count, 0)
    inward = jnp.einsum("qg,qisx->igsx", selector, received, precision=exact_mode).reshape(
        9, beside_all, axial
    )
    low_first = jnp.where(annulus, inward, mirrored(padded_first, beside_all, axial))
    high_first = jnp.where(annulus, bounced(post_first), inward)
    middle = stream(padded_first, low_first, high_first, beside_all, axial)
    post_second, padded_second = advance(middle, second_collision)
    finished = stream(padded_second, inward, bounced(post_second), beside_all, axial)
    return jnp.where(annulus, finished, middle)[None]


def solution(mesh):
    in_specs = (P("grp", None, None, "az", "ax"), P(), P("ax", None))
    out_specs = P("grp", None, None, "az", "ax")
    return jax.shard_map(local, mesh=mesh, in_specs=in_specs, out_specs=out_specs, check_vma=False)
```

profile of v0, /device:TPU:0, one launch (start us, length us, event | category | flops | bytes accessed | tf_op | source)
XLA Modules:
  0.0 63.5 jit_solution(18248365676939347525)
XLA Ops:
  0.0 2.3 %fusion.5 = f32[1,2,32,128]{3,0,2,1:T(1,128)S(1)} fusion(f32[27,1,1,1]{0,1,3,2:T(1,128)} %constant.77, f32[27,2,32,128]{3,2,1,0:T(8,128)} %bitcast.493), kind=kOutput, calls=%fused_computation.13 | convolution fusion | flops 2654208 | bytes 917612 | tf_op jit(solution)/shard_map/i,i...->.../dot_general | solution.py:85
  2.3 2.4 %multiply_reduce_fusion.1 = (f32[2,32,128]{2,1,0:T(8,128)S(1)}, f32[3,2,32,128]{3,0,2,1:T(4,128)S(1)}) fusion(f32[2,32,128]{2,1,0:T(8,128)S(1)} %bitcast.495, f32[27,3,1,1]{0,1,3,2:T(4,128)S(1)} %copy-done.22, f32[27,2,32,128]{3,2,1,0:T(8,128)} %bitcast.494), kind=kOutput, calls=%fused_computation.157 | convolution fusion | flops 8028160 | bytes 1048900 | tf_op jit(solution)/shard_map/ik,i...->k.../dot_general | solution.py:86
  4.8 1.1 %fusion.69 = f32[27,2,32,128]{3,0,2,1:T(8,128)S(1)} fusion(f32[27,3,1,1]{0,1,3,2:T(4,128)S(1)} %copy-done.21, f32[3,2,32,128]{3,0,2,1:T(4,128)S(1)} %get-tuple-element.127), kind=kOutput, calls=%fused_computation.331 | convolution fusion | flops 7962624 | bytes 983364 | tf_op jit(solution)/shard_map/ik,k...->i.../dot_general | solution.py:87
  5.9 0.6 fusion.15
  6.5 0.1 copy-done.19
  6.6 0.2 fusion.38
  6.7 0.6 copy-done.17
  7.3 1.5 %fusion.10 = f32[27,2,32,128]{3,0,2,1:T(8,128)S(1)} fusion(f32[27,2,32,128]{3,2,1,0:T(8,128)S(1)} %fusion.15, f32[2,27,27]{2,1,0:T(8,128)S(1)} %fusion.38, s32[]{:T(128)S(6)} %select_n.65), kind=kOutput, calls=%fused_computation.18 | convolution fusion | flops 71663616 | bytes 1785860 | tf_op jit(solution)/shard_map/ij,j...->i.../dot_general | solution.py:93
  8.9 0.5 copy_subtract_fusion.1
  9.5 0.5 collective-permute-start
  10.0 2.0 %collective-permute-start.1 = (f32[27,2,1,128]{3,2,1,0:T(1,128)S(1)}, f32[27,2,1,128]{3,2,1,0:T(1,128)S(1)}, u32[]{:S(2)}, u32[]{:S(2)}) collective-permute-start(f32[27,2,1,128]{3,2,1,0:T(1,128)S(1)} %get-tuple-element.94), channel_id=1, source_target_pairs={{4,0},{8,4},{12,8},{0,12},{5,1},{9,5},{13,9},{1,13},{6,2},{10,6},{... | collective-permute-start | bytes 82952 | tf_op jit(solution)/shard_map/ppermute | solution.py:17
  11.9 0.6 %fusion.68 = (f32[1,1]{1,0:T(1,128)}, f32[1,1]{1,0:T(1,128)}) fusion(f32[2,27]{1,0:T(2,128)S(1)} %copy-done.24), kind=kLoop, calls=%fused_computation.330 | loop fusion | bytes 16 | tf_op jit(solution)/shard_map/slice | solution.py:150
  14.7 0.5 copy-done.28
  15.2 0.7 %fusion.20 = f32[1,32,128]{2,0,1:T(1,128)S(1)} fusion(f32[27,1,1]{0,1,2:T(1,128)S(1)} %copy-done.28, f32[27,32,128]{2,1,0:T(8,128)S(1)} %fusion.85), kind=kOutput, calls=%fused_computation.31 | convolution fusion | flops 1327104 | bytes 458860 | tf_op jit(solution)/shard_map/i,i...->.../dot_general | solution.py:85
  15.9 0.7 %multiply_reduce_fusion.2 = (f32[32,128]{1,0:T(8,128)S(1)}, f32[3,32,128]{2,0,1:T(4,128)S(1)}) fusion(f32[32,128]{1,0:T(8,128)S(1)} %bitcast.499, f32[27,3,1]{0,1,2:T(4,128)S(1)} %copy-done.26, f32[27,32,128]{2,1,0:T(8,128)S(1)} %fusion.85), kind=kOutput, calls=%fused_computation.158 | convolution fusion | flops 4014080 | bytes 524612 | tf_op jit(solution)/shard_map/ik,i...->k.../dot_general | solution.py:86
  16.6 0.6 %fusion.70 = f32[27,32,128]{2,0,1:T(8,128)S(1)} fusion(f32[27,3,1]{0,1,2:T(4,128)S(1)} %copy-done.25, f32[3,32,128]{2,0,1:T(4,128)S(1)} %get-tuple-element.129), kind=kOutput, calls=%fused_computation.332 | convolution fusion | flops 3981312 | bytes 491844 | tf_op jit(solution)/shard_map/ik,k...->i.../dot_general | solution.py:87
  17.3 0.3 fusion.25
  17.7 0.5 copy-done.23
  18.2 0.4 fusion.36
  18.6 0.8 %copy.134 = f32[8,9,8,128]{3,2,1,0:T(8,128)} copy(f32[8,9,8,128]{3,0,2,1:T(8,128)S(1)} %pad_select_fusion) | data formatting | bytes 589824 | tf_op jit(solution)/shard_map/jit(_where)/select_n | solution.py:177
  19.4 4.5 %all-to-all-start = ((f32[8,9,8,128]{3,2,1,0:T(8,128)}), f32[8,9,8,128]{3,2,1,0:T(8,128)S(1)}, u32[]{:S(2)}, u32[]{:S(2)}) async-start(f32[8,9,8,128]{3,2,1,0:T(8,128)} %copy.134), calls=%async_computation | async-start | bytes 589824 | tf_op jit(solution)/shard_map/all_to_all | solution.py:182
  23.9 0.2 pad_maximum_fusion
  24.0 0.4 fusion.62
  24.4 0.5 copy.137
  24.9 0.5 copy.124
  25.3 3.7 %collective-permute-start.2 = (f32[27,2,34,1]{2,1,3,0:T(2,128)S(1)}, f32[27,2,34,1]{2,1,3,0:T(2,128)S(1)}, u32[]{:S(2)}, u32[]{:S(2)}) collective-permute-start(f32[27,2,34,1]{2,1,3,0:T(2,128)S(1)} %copy.124), channel_id=1, source_target_pairs={{1,0},{2,1},{3,2},{0,3},{5,4},{6,5},{7,6},{4,7},{9,8},{10,9},{11,1... | collective-permute-start | bytes 22040 | tf_op jit(solution)/shard_map/ppermute | solution.py:17
  29.0 0.6 maximum_bitcast_fusion.56
  29.6 5.0 %collective-permute-done.3 = f32[27,2,34,1]{2,1,3,0:T(2,128)S(1)} collective-permute-done((f32[27,2,34,1]{2,1,3,0:T(2,128)S(1)}, f32[27,2,34,1]{2,1,3,0:T(2,128)S(1)}, u32[]{:S(2)}, u32[]{:S(2)}) %collective-permute-start.3) | collective-permute-done | bytes 7376 | tf_op jit(solution)/shard_map/ppermute | solution.py:16
  34.6 0.5 copy.138
  35.1 0.5 copy.125
  35.9 0.7 %fusion.45 = (f32[1,32,128]{2,1,0:T(8,128)S(1)}, f32[1,32,128]{2,1,0:T(8,128)S(1)}, f32[1,32,128]{2,1,0:T(8,128)S(1)}, f32[1,32,128]{2,1,0:T(8,128)}, f32[1,32,128]{2,1,0:T(8,128)}, /*index=5*/f32[1,32,128]{2,1,0:T(8,128)}) fusion(f32[27,2,34,1]{3,2,1,0:T(8,128)S(1)} %copy.138, f32[27,2,1,128]{3,2,1,0:T(1,128)S(1)} %collective-permute-done.1, ...), kind=kLoop, calls=%fused_computation.252 | loop fusion | flops 53248 | bytes 2160640 | tf_op jit(solution)/shard_map/slice | solution.py:111
  36.9 0.7 %maximum_bitcast_fusion.53 = (f32[1,32,128]{2,1,0:T(8,128)}, f32[1,32,128]{2,1,0:T(8,128)}, f32[1,32,128]{2,1,0:T(8,128)}, f32[1,32,128]{2,1,0:T(8,128)}, f32[1,32,128]{2,1,0:T(8,128)S(1)}) fusion(f32[27,2,34,1]{3,2,1,0:T(8,128)S(1)} %copy.138, f32[27,2,1,128]{3,2,1,0:T(1,128)S(1)} %collective-permute-done.1, ...), kind=kLoop, calls=%fused_computation.280 | loop fusion | flops 53248 | bytes 1036640 | tf_op jit(solution)/shard_map/slice | solution.py:113
  37.6 0.7 %fusion.47 = (f32[1,32,128]{2,1,0:T(8,128)S(1)}, f32[1,32,128]{2,1,0:T(8,128)}, f32[1,32,128]{2,1,0:T(8,128)}, f32[1,32,128]{2,1,0:T(8,128)}, f32[1,32,128]{2,1,0:T(8,128)}, /*index=5*/f32[1,32,128]{2,1,0:T(8,128)S(1)}) fusion(f32[27,2,34,1]{3,2,1,0:T(8,128)S(1)} %copy.125, f32[27,2,1,128]{3,2,1,0:T(1,128)S(1)} %collective-permute-done.1, ...), kind=kLoop, calls=%fused_computation.258 | loop fusion | flops 53248 | bytes 2160640 | tf_op jit(solution)/shard_map/slice | solution.py:111
  38.4 1.0 %convolution_bitcast_fusion = f32[9,4,8,128]{3,1,2,0:T(4,128)S(1)} fusion(f32[4,9,8,128]{3,2,1,0:T(8,128)S(1)} %constant_dynamic-slice_fusion, s32[4]{0:T(128)} %copy-done.23), kind=kOutput, calls=%fused_computation.2 | convolution fusion | flops 1769488 | bytes 294928 | tf_op jit(solution)/shard_map/qg,qisx->igsx/dot_general | solution.py:184
  39.4 1.0 %bitcast_select_fusion = (f32[9,32,128]{2,1,0:T(8,128)S(1)}, f32[9,32,128]{2,1,0:T(8,128)S(1)}) fusion(f32[9,32,128]{2,1,0:T(8,128)} %copy-done.3, f32[9,4,8,128]{3,1,2,0:T(4,128)S(1)} %convolution_bitcast_fusion, pred[]{:T(512)S(6)} %eq.20, f32[9,32,128]{2,1,0:T(8,128)} %copy-done.4), kind=kLoop, calls=%fused_computation.152 | loop fusion | flops 73728 | bytes 737281 | tf_op jit(solution)/shard_map/jit(_where)/select_n | solution.py:187
  40.6 0.1 constant_dynamic-update-slice_fusion.89
  40.8 0.1 constant_dynamic-update-slice_fusion.86
  41.2 0.1 constant_dynamic-update-slice_fusion.83
  41.5 0.6 copy-done.7
  42.3 1.2 %fusion.2 = f32[1,2,32,128]{3,0,2,1:T(1,128)S(1)} fusion(f32[27,1,1,1]{0,1,3,2:T(1,128)S(1)} %copy-done.27, f32[27,2,32,128]{3,2,1,0:T(8,128)S(1)} %constant_dynamic-update-slice_fusion.18), kind=kOutput, calls=%fused_computation.10 | convolution fusion | flops 2654208 | bytes 917612 | tf_op jit(solution)/shard_map/i,i...->.../dot_general | solution.py:85
  43.5 1.3 %multiply_reduce_fusion = (f32[2,32,128]{2,1,0:T(8,128)S(1)}, f32[3,2,32,128]{3,0,2,1:T(4,128)S(1)}) fusion(f32[2,32,128]{2,1,0:T(8,128)S(1)} %bitcast.497, f32[27,3,1,1]{0,1,3,2:T(4,128)S(1)} %copy-done.22, f32[27,2,32,128]{3,2,1,0:T(8,128)S(1)} %constant_dynamic-update-slice_fusion.18), kind=kOutput, calls=%fused_computation.156 | convolution fusion | flops 8028160 | bytes 1048900 | tf_op jit(solution)/shard_map/ik,i...->k.../dot_general | solution.py:86
  44.8 1.1 %fusion.71 = f32[27,2,32,128]{3,0,2,1:T(8,128)S(1)} fusion(f32[27,3,1,1]{0,1,3,2:T(4,128)S(1)} %copy-done.21, f32[3,2,32,128]{3,0,2,1:T(4,128)S(1)} %get-tuple-element.131), kind=kOutput, calls=%fused_computation.333 | convolution fusion | flops 7962624 | bytes 983364 | tf_op jit(solution)/shard_map/ik,k...->i.../dot_general | solution.py:87
  45.9 0.6 fusion.19
  46.5 0.1 copy-done.18
  46.7 1.5 %fusion.8 = f32[27,2,32,128]{3,0,2,1:T(8,128)S(1)} fusion(f32[27,2,32,128]{3,2,1,0:T(8,128)S(1)} %fusion.19, f32[2,27,27]{2,1,0:T(8,128)S(1)} %copy-done.18), kind=kOutput, calls=%fused_computation.16 | convolution fusion | flops 71663616 | bytes 1785856 | tf_op jit(solution)/shard_map/ij,j...->i.../dot_general | solution.py:93
  48.2 0.5 copy_subtract_fusion
  48.8 1.7 %collective-permute-start.5 = (f32[27,2,1,128]{3,2,1,0:T(1,128)S(1)}, f32[27,2,1,128]{3,2,1,0:T(1,128)S(1)}, u32[]{:S(2)}, u32[]{:S(2)}) collective-permute-start(f32[27,2,1,128]{3,2,1,0:T(1,128)S(1)} %get-tuple-element.72), channel_id=1, source_target_pairs={{4,0},{8,4},{12,8},{0,12},{5,1},{9,5},{13,9},{1,13},{6,2},{10,6},{... | collective-permute-start | bytes 82952 | tf_op jit(solution)/shard_map/ppermute | solution.py:17
  50.6 1.5 %collective-permute-done.4 = f32[27,2,1,128]{3,2,1,0:T(1,128)S(1)} collective-permute-done((f32[27,2,1,128]{3,2,1,0:T(1,128)S(1)}, f32[27,2,1,128]{3,2,1,0:T(1,128)S(1)}, u32[]{:S(2)}, u32[]{:S(2)}) %collective-permute-start.4) | collective-permute-done | bytes 27680 | tf_op jit(solution)/shard_map/ppermute | solution.py:16
  52.1 0.2 pad_maximum_fusion.1
  52.3 0.4 fusion.61
  52.6 0.5 copy.147
  53.1 0.5 copy.145
  53.6 2.0 %collective-permute-start.7 = (f32[27,2,34,1]{2,1,3,0:T(2,128)S(1)}, f32[27,2,34,1]{2,1,3,0:T(2,128)S(1)}, u32[]{:S(2)}, u32[]{:S(2)}) collective-permute-start(f32[27,2,34,1]{2,1,3,0:T(2,128)S(1)} %copy.147), channel_id=1, source_target_pairs={{0,1},{1,2},{2,3},{3,0},{4,5},{5,6},{6,7},{7,4},{8,9},{9,10},{10,1... | collective-permute-start | bytes 22040 | tf_op jit(solution)/shard_map/ppermute | solution.py:16
  55.7 3.7 %collective-permute-done.7 = f32[27,2,34,1]{2,1,3,0:T(2,128)S(1)} collective-permute-done((f32[27,2,34,1]{2,1,3,0:T(2,128)S(1)}, f32[27,2,34,1]{2,1,3,0:T(2,128)S(1)}, u32[]{:S(2)}, u32[]{:S(2)}) %collective-permute-start.7) | collective-permute-done | bytes 7376 | tf_op jit(solution)/shard_map/ppermute | solution.py:16
  59.3 0.5 copy.148
  59.9 0.5 copy.146
  60.4 0.1 maximum_bitcast_fusion.33
  60.5 0.1 fusion.43
  60.7 0.1 fusion.41
  60.8 0.1 constant_dynamic-update-slice_fusion.62
  61.0 0.1 constant_dynamic-update-slice_fusion.59
  61.2 0.1 constant_dynamic-update-slice_fusion.56
  61.5 1.0 %copy-done.2 = f32[1,27,2,32,128]{4,3,2,1,0:T(8,128)S(1)} copy-done((f32[1,27,2,32,128]{4,3,2,1,0:T(8,128)S(1)}, f32[1,27,2,32,128]{4,3,2,1,0:T(8,128)}, u32[]{:S(2)}) %copy-start.2) | copy-done | bytes 884760
  62.5 1.1 %broadcast_select_fusion = f32[1,27,2,32,128]{4,3,2,1,0:T(8,128)} fusion(f32[1,27,2,32,128]{4,3,2,1,0:T(8,128)S(1)} %constant_dynamic-update-slice_fusion.45, f32[1,27,2,32,128]{4,3,2,1,0:T(8,128)S(1)} %copy-done.2, pred[]{:T(512)S(6)} %eq.20), kind=kLoop, calls=%fused_computation.40 | loop fusion | flops 221184 | bytes 2654209 | tf_op jit(solution)/shard_map/jit(_where)/select_n | solution.py:192
  (168 shorter events, 2.1 us)
Async XLA Ops:
  0.0 2.3 %copy-start.22 = (f32[27,3,1,1]{0,1,3,2:T(4,128)S(1)}, f32[27,3,1,1]{0,1,3,2:T(4,128)}, u32[]{:S(2)}) copy-start(f32[27,3,1,1]{0,1,3,2:T(4,128)} %constant.79) | copy-start | bytes 976
  0.0 4.7 %copy-start.24 = (f32[2,27]{1,0:T(2,128)S(1)}, f32[2,27]{1,0:T(2,128)}, u32[]{:S(2)}) copy-start(f32[2,27]{1,0:T(2,128)} %param.16) | copy-start | bytes 652
  0.0 4.7 %copy-start.29 = (f32[27]{0:T(128)S(1)}, f32[27]{0:T(128)}, u32[]{:S(2)}) copy-start(f32[27]{0:T(128)} %constant.65.clone) | copy-start | bytes 328
  0.0 4.7 %copy-start.21 = (f32[27,3,1,1]{0,1,3,2:T(4,128)S(1)}, f32[27,3,1,1]{0,1,3,2:T(4,128)}, u32[]{:S(2)}) copy-start(f32[27,3,1,1]{0,1,3,2:T(4,128)} %constant.78) | copy-start | bytes 976
  2.3 3.5 %copy-start = (f32[1,27,2,32,128]{4,3,2,1,0:T(8,128)S(1)}, f32[1,27,2,32,128]{4,3,2,1,0:T(8,128)}, u32[]{:S(2)}) copy-start(f32[1,27,2,32,128]{4,3,2,1,0:T(8,128)} %param.15) | copy-start | bytes 2654212
  5.8 0.7 %copy-start.19 = (f32[27,27,1]{1,0,2:T(8,128)S(1)}, f32[27,27,1]{1,0,2:T(8,128)}, u32[]{:S(2)}) copy-start(f32[27,27,1]{1,0,2:T(8,128)} %constant.76) | copy-start | bytes 8752
  5.8 0.7 %copy-start.20 = (f32[27,27]{0,1:T(8,128)S(1)}, f32[27,27]{0,1:T(8,128)}, u32[]{:S(2)}) copy-start(f32[27,27]{0,1:T(8,128)} %constant.75) | copy-start | bytes 8752
  6.7 0.6 copy-start.17
  9.5 14.4 %collective-permute-start = (f32[27,2,1,128]{3,2,1,0:T(1,128)S(1)}, f32[27,2,1,128]{3,2,1,0:T(1,128)S(1)}, u32[]{:S(2)}, u32[]{:S(2)}) collective-permute-start(f32[27,2,1,128]{3,2,1,0:T(1,128)S(1)} %get-tuple-element.93), channel_id=1, source_target_pairs={{0,4},{4,8},{8,12},{12,0},{1,5},{5,9},{9,13},{13,1},{2,6},{6,10},{... | collective-permute-start | bytes 82952 | tf_op jit(solution)/shard_map/ppermute | solution.py:16
  10.0 13.9 %collective-permute-start.1 = (f32[27,2,1,128]{3,2,1,0:T(1,128)S(1)}, f32[27,2,1,128]{3,2,1,0:T(1,128)S(1)}, u32[]{:S(2)}, u32[]{:S(2)}) collective-permute-start(f32[27,2,1,128]{3,2,1,0:T(1,128)S(1)} %get-tuple-element.94), channel_id=1, source_target_pairs={{4,0},{8,4},{12,8},{0,12},{5,1},{9,5},{13,9},{1,13},{6,2},{10,6},{... | collective-permute-start | bytes 82952 | tf_op jit(solution)/shard_map/ppermute | solution.py:17
  14.5 0.7 %copy-start.28 = (f32[27,1,1]{0,1,2:T(1,128)S(1)}, f32[27,1,1]{0,1,2:T(1,128)}, u32[]{:S(2)}) copy-start(f32[27,1,1]{0,1,2:T(1,128)} %constant.80) | copy-start | bytes 328
  14.6 1.3 %copy-start.26 = (f32[27,3,1]{0,1,2:T(4,128)S(1)}, f32[27,3,1]{0,1,2:T(4,128)}, u32[]{:S(2)}) copy-start(f32[27,3,1]{0,1,2:T(4,128)} %constant.82) | copy-start | bytes 976
  14.6 2.0 %copy-start.25 = (f32[27,3,1]{0,1,2:T(4,128)S(1)}, f32[27,3,1]{0,1,2:T(4,128)}, u32[]{:S(2)}) copy-start(f32[27,3,1]{0,1,2:T(4,128)} %constant.81) | copy-start | bytes 976
  15.9 1.7 %copy-start.30 = (s32[1,4]{1,0:T(1,128)S(1)}, s32[1,4]{1,0:T(1,128)}, u32[]{:S(2)}) copy-start(s32[1,4]{1,0:T(1,128)} %param.17) | copy-start | bytes 52
  17.6 0.5 copy-start.23
  19.4 18.9 %all-to-all-start = ((f32[8,9,8,128]{3,2,1,0:T(8,128)}), f32[8,9,8,128]{3,2,1,0:T(8,128)S(1)}, u32[]{:S(2)}, u32[]{:S(2)}) async-start(f32[8,9,8,128]{3,2,1,0:T(8,128)} %copy.134), calls=%async_computation | async-start | bytes 589824 | tf_op jit(solution)/shard_map/all_to_all | solution.py:182
  25.3 9.8 %collective-permute-start.2 = (f32[27,2,34,1]{2,1,3,0:T(2,128)S(1)}, f32[27,2,34,1]{2,1,3,0:T(2,128)S(1)}, u32[]{:S(2)}, u32[]{:S(2)}) collective-permute-start(f32[27,2,34,1]{2,1,3,0:T(2,128)S(1)} %copy.124), channel_id=1, source_target_pairs={{1,0},{2,1},{3,2},{0,3},{5,4},{6,5},{7,6},{4,7},{9,8},{10,9},{11,1... | collective-permute-start | bytes 22040 | tf_op jit(solution)/shard_map/ppermute | solution.py:17
  29.0 5.7 %collective-permute-start.3 = (f32[27,2,34,1]{2,1,3,0:T(2,128)S(1)}, f32[27,2,34,1]{2,1,3,0:T(2,128)S(1)}, u32[]{:S(2)}, u32[]{:S(2)}) collective-permute-start(f32[27,2,34,1]{2,1,3,0:T(2,128)S(1)} %copy.137), channel_id=1, source_target_pairs={{0,1},{1,2},{2,3},{3,0},{4,5},{5,6},{6,7},{7,4},{8,9},{9,10},{10,1... | collective-permute-start | bytes 22040 | tf_op jit(solution)/shard_map/ppermute | solution.py:16
  36.8 0.7 %copy-start.3 = (f32[9,32,128]{2,1,0:T(8,128)}, f32[9,32,128]{2,1,0:T(8,128)S(1)}, u32[]{:S(2)}) copy-start(f32[9,32,128]{2,1,0:T(8,128)S(1)} %get-tuple-element.75) | copy-start | bytes 442372
  36.8 0.7 %copy-start.4 = (f32[9,32,128]{2,1,0:T(8,128)}, f32[9,32,128]{2,1,0:T(8,128)S(1)}, u32[]{:S(2)}) copy-start(f32[9,32,128]{2,1,0:T(8,128)S(1)} %get-tuple-element.76) | copy-start | bytes 442372
  38.3 2.1 %copy-start.16 = (f32[1,32,128]{2,1,0:T(8,128)S(1)}, f32[1,32,128]{2,1,0:T(8,128)}, u32[]{:S(2)}) copy-start(f32[1,32,128]{2,1,0:T(8,128)} %get-tuple-element.51) | copy-start | bytes 49156
  38.3 2.1 %copy-start.8 = (f32[1,32,128]{2,1,0:T(8,128)S(1)}, f32[1,32,128]{2,1,0:T(8,128)}, u32[]{:S(2)}) copy-start(f32[1,32,128]{2,1,0:T(8,128)} %maximum_bitcast_fusion.56) | copy-start | bytes 49156
  38.3 2.1 %copy-start.15 = (f32[1,32,128]{2,1,0:T(8,128)S(1)}, f32[1,32,128]{2,1,0:T(8,128)}, u32[]{:S(2)}) copy-start(f32[1,32,128]{2,1,0:T(8,128)} %get-tuple-element.42) | copy-start | bytes 49156
  38.4 2.1 %copy-start.14 = (f32[1,32,128]{2,1,0:T(8,128)S(1)}, f32[1,32,128]{2,1,0:T(8,128)}, u32[]{:S(2)}) copy-start(f32[1,32,128]{2,1,0:T(8,128)} %get-tuple-element.52) | copy-start | bytes 49156
  38.4 2.1 %copy-start.11 = (f32[1,32,128]{2,1,0:T(8,128)S(1)}, f32[1,32,128]{2,1,0:T(8,128)}, u32[]{:S(2)}) copy-start(f32[1,32,128]{2,1,0:T(8,128)} %get-tuple-element.73) | copy-start | bytes 49156
  38.4 2.2 %copy-start.13 = (f32[1,32,128]{2,1,0:T(8,128)S(1)}, f32[1,32,128]{2,1,0:T(8,128)}, u32[]{:S(2)}) copy-start(f32[1,32,128]{2,1,0:T(8,128)} %get-tuple-element.41) | copy-start | bytes 49156
  39.4 1.2 %copy-start.12 = (f32[1,32,128]{2,1,0:T(8,128)S(1)}, f32[1,32,128]{2,1,0:T(8,128)}, u32[]{:S(2)}) copy-start(f32[1,32,128]{2,1,0:T(8,128)} %get-tuple-element.40) | copy-start | bytes 49156
  39.4 1.2 %copy-start.10 = (f32[1,32,128]{2,1,0:T(8,128)S(1)}, f32[1,32,128]{2,1,0:T(8,128)}, u32[]{:S(2)}) copy-start(f32[1,32,128]{2,1,0:T(8,128)} %get-tuple-element.56) | copy-start | bytes 49156
  39.4 1.2 %copy-start.9 = (f32[1,32,128]{2,1,0:T(8,128)S(1)}, f32[1,32,128]{2,1,0:T(8,128)}, u32[]{:S(2)}) copy-start(f32[1,32,128]{2,1,0:T(8,128)} %get-tuple-element.36) | copy-start | bytes 49156
  41.3 0.7 %copy-start.7 = (f32[1,32,128]{2,1,0:T(8,128)S(1)}, f32[1,32,128]{2,1,0:T(8,128)}, u32[]{:S(2)}) copy-start(f32[1,32,128]{2,1,0:T(8,128)} %get-tuple-element.39) | copy-start | bytes 49156
  41.3 0.7 %copy-start.6 = (f32[1,32,128]{2,1,0:T(8,128)S(1)}, f32[1,32,128]{2,1,0:T(8,128)}, u32[]{:S(2)}) copy-start(f32[1,32,128]{2,1,0:T(8,128)} %get-tuple-element.58) | copy-start | bytes 49156
  41.3 0.8 %copy-start.5 = (f32[1,32,128]{2,1,0:T(8,128)S(1)}, f32[1,32,128]{2,1,0:T(8,128)}, u32[]{:S(2)}) copy-start(f32[1,32,128]{2,1,0:T(8,128)} %get-tuple-element.38) | copy-start | bytes 49156
  41.4 0.8 %copy-start.27 = (f32[27,1,1,1]{0,1,3,2:T(1,128)S(1)}, f32[27,1,1,1]{0,1,3,2:T(1,128)}, u32[]{:S(2)}) copy-start(f32[27,1,1,1]{0,1,3,2:T(1,128)} %constant.77) | copy-start | bytes 328
  45.9 0.8 %copy-start.18 = (f32[2,27,27]{2,1,0:T(8,128)S(1)}, f32[2,27,27]{2,1,0:T(8,128)}, u32[]{:S(2)}) copy-start(f32[2,27,27]{2,1,0:T(8,128)} %copy-done.17) | copy-start | bytes 17500
  48.8 3.3 %collective-permute-start.4 = (f32[27,2,1,128]{3,2,1,0:T(1,128)S(1)}, f32[27,2,1,128]{3,2,1,0:T(1,128)S(1)}, u32[]{:S(2)}, u32[]{:S(2)}) collective-permute-start(f32[27,2,1,128]{3,2,1,0:T(1,128)S(1)} %get-tuple-element.71), channel_id=1, source_target_pairs={{0,4},{4,8},{8,12},{12,0},{1,5},{5,9},{9,13},{13,1},{2,6},{6,10},{... | collective-permute-start | bytes 82952 | tf_op jit(solution)/shard_map/ppermute | solution.py:16
  48.8 3.3 %collective-permute-start.5 = (f32[27,2,1,128]{3,2,1,0:T(1,128)S(1)}, f32[27,2,1,128]{3,2,1,0:T(1,128)S(1)}, u32[]{:S(2)}, u32[]{:S(2)}) collective-permute-start(f32[27,2,1,128]{3,2,1,0:T(1,128)S(1)} %get-tuple-element.72), channel_id=1, source_target_pairs={{4,0},{8,4},{12,8},{0,12},{5,1},{9,5},{13,9},{1,13},{6,2},{10,6},{... | collective-permute-start | bytes 82952 | tf_op jit(solution)/shard_map/ppermute | solution.py:17
  50.6 1.5 %copy-start.1 = (f32[1,27,2,32,128]{4,3,2,1,0:T(8,128)}, f32[1,27,2,32,128]{4,3,2,1,0:T(8,128)S(1)}, u32[]{:S(2)}) copy-start(f32[1,27,2,32,128]{4,3,2,1,0:T(8,128)S(1)} %constant_dynamic-update-slice_fusion.72) | copy-start | bytes 2654212
  53.6 6.3 %collective-permute-start.6 = (f32[27,2,34,1]{2,1,3,0:T(2,128)S(1)}, f32[27,2,34,1]{2,1,3,0:T(2,128)S(1)}, u32[]{:S(2)}, u32[]{:S(2)}) collective-permute-start(f32[27,2,34,1]{2,1,3,0:T(2,128)S(1)} %copy.145), channel_id=1, source_target_pairs={{1,0},{2,1},{3,2},{0,3},{5,4},{6,5},{7,6},{4,7},{9,8},{10,9},{11,1... | collective-permute-start | bytes 22040 | tf_op jit(solution)/shard_map/ppermute | solution.py:17
  53.6 5.7 %collective-permute-start.7 = (f32[27,2,34,1]{2,1,3,0:T(2,128)S(1)}, f32[27,2,34,1]{2,1,3,0:T(2,128)S(1)}, u32[]{:S(2)}, u32[]{:S(2)}) collective-permute-start(f32[27,2,34,1]{2,1,3,0:T(2,128)S(1)} %copy.147), channel_id=1, source_target_pairs={{0,1},{1,2},{2,3},{3,0},{4,5},{5,6},{6,7},{7,4},{8,9},{9,10},{10,1... | collective-permute-start | bytes 22040 | tf_op jit(solution)/shard_map/ppermute | solution.py:16
  61.3 1.2 %copy-start.2 = (f32[1,27,2,32,128]{4,3,2,1,0:T(8,128)S(1)}, f32[1,27,2,32,128]{4,3,2,1,0:T(8,128)}, u32[]{:S(2)}) copy-start(f32[1,27,2,32,128]{4,3,2,1,0:T(8,128)} %copy-done.1) | copy-start | bytes 2654212
where the time goes:
time: 64.7 us; the launch traced here: 63.5 us
  matrix products  15.9 us (25%)
  starting transfers between devices  14.5 us (22%)
  waiting for transfers between devices  10.2 us (16%)
  other arithmetic  10.1 us (16%)
  local copies, waits for them, and re-layouts  9.68 us (15%)
  between operations  3.25 us (5%)
    ppermute x4, waiting for transfers between devices, padded_2(): before = lax.ppermute(last, axis, up)  10.2 us
    ppermute x4, starting transfers between devices, padded_2(): after = lax.ppermute(first, axis, down)  7.43 us
    all_to_all x1, starting transfers between devices, local(): lax.all_to_all(stacked, ('grp', 'az'), split_axis=0, concat_axis=0, tiled...  4.48 us
    dot_general x3, matrix products, equilibrium(): jnp.einsum('ik,i...->k...', drift_table, state, precision=exact_mode)  4.36 us
    dot_general x3, matrix products, equilibrium(): jnp.einsum('i,i...->...', weight_table, state, precision=exact_mode)  4.23 us
    unnamed x74, local copies, waits for them, and re-layouts  3.5 us
    dot_general x2, matrix products, relax(): jnp.einsum('ij,j...->i...', collision_matrix, state - equilibrium(state),...  3.02 us
    dot_general x3, matrix products, equilibrium(): jnp.einsum('ik,k...->i...', speed_table, flow, precision=exact_mode)  2.76 us
  transfers between devices with their start and end apart: 9, of which 3 were waited for; matrix products, arithmetic and copies ran while one was open for 17% of the time, Pallas kernels for 0%

commit v1 on v0

v1 whole, which is shorter than its diff:
```python
import functools

import jax
import jax.numpy as jnp
from jax import lax
from jax.experimental import pallas as pl
from jax.experimental.pallas import tpu as pltpu
from jax.sharding import PartitionSpec as P

TILE = 8
COMBOS = ((0, 0), (1, 0), (0, 1), (-1, 1), (-1, 0))
FIXED = (0, 1, 3, 9)


def velocity(radial, around, along):
    return 9 * (radial + 1) + 3 * (around + 1) + (along + 1)


def triples():
    for stride in (9, 3, 1):
        for base in range(27):
            if base // stride % 3 == 0:
                yield base, base + stride, base + 2 * stride


def moments_of(state):
    x = list(state)
    for low, mid, high in triples():
        even = x[high] + x[low]
        x[low], x[mid], x[high] = even + 4.0 * x[mid], x[high] - x[low], even
    return x


def populations_of(scaled):
    x = list(scaled)
    for low, mid, high in triples():
        zero, one, two = x[low], x[mid], x[high]
        half = 0.5 * two
        x[mid] = -half if zero is None else zero - half
        x[high] = two if one is None else two + one
        x[low] = two if one is None else two - one
    return x


def flow_of(moment):
    density = moment[0]
    drift = (moment[9], moment[3], moment[1])
    inverse = 1.0 / density
    speed = tuple(j * inverse for j in drift)
    return density, drift, speed


def collide(state, rate):
    moment = moments_of(state)
    density, drift, speed = flow = flow_of(moment)
    square = [drift[d] * speed[d] for d in range(3)]
    scaled = []
    for index in range(27):
        if index in FIXED:
            scaled.append(None)
            continue
        power = (index // 9, index // 3 % 3, index % 3)
        odd = [d for d in range(3) if power[d] == 1]
        two = [d for d in range(3) if power[d] == 2]
        third = (1.0 / 3.0) ** len(two)
        if len(odd) == 0:
            total = functools.reduce(lambda a, b: a + b, [square[d] for d in two])
            balance = density * third + total * (3.0 * third)
        elif len(odd) == 1:
            balance = drift[odd[0]] * third
        elif len(odd) == 2:
            balance = drift[odd[0]] * speed[odd[1]] * third
        else:
            balance = None
        off = moment[index] if balance is None else moment[index] - balance
        scaled.append(off * rate[index])
    change = populations_of(scaled)
    return [g - c for g, c in zip(state, change)], flow


def scaled_rates(rates_ref, group):
    out = []
    for index in range(27):
        power = (index // 9, index // 3 % 3, index % 3)
        scale = 1.0
        for p in power:
            scale *= 0.25 if p == 0 else 0.5
        out.append(None if index in FIXED else rates_ref[group, index] * scale)
    return out


def kernel(
    count,
    length,
    pop_ref,
    rates_ref,
    offset_ref,
    out_ref,
    source,
    first,
    second,
    result,
    outward,
    tile_send,
    tile_recv,
    ghost,
    row_send,
    row_recv,
    col_send,
    col_recv,
    load_sem,
    store_sem,
    tile_send_sem,
    tile_recv_sem,
    edge_send_sem,
    edge_recv_sem,
):
    rows = source.shape[2]
    cells = source.shape[3]
    slots = rows // count
    tiles = rows // TILE
    group = lax.axis_index("grp")
    place = lax.axis_index("az")
    block = lax.axis_index("ax")
    annulus = group == 0
    face = group
    back = 1 - group

    loads = [
        pltpu.make_async_copy(pop_ref.at[0, :, r], source.at[:, r], load_sem.at[k])
        for k, r in enumerate((face, back))
    ]
    for copy in loads:
        copy.start()

    def device(around, along):
        return {
            "grp": group,
            "az": lax.rem(place + around + count, count),
            "ax": lax.rem(block + along + length, length),
        }

    def across(position):
        return {"grp": 1 - group, "az": position, "ax": block}

    barrier = pltpu.get_barrier_semaphore()
    sides = [(i, j) for i in (-1, 0, 1) for j in (-1, 0, 1) if (i, j) != (0, 0)]
    for i, j in sides:
        pl.semaphore_signal(barrier, 1, device_id=device(i, j), device_id_type=pl.DeviceIdType.MESH)
    for d in range(count):
        pl.semaphore_signal(barrier, 1, device_id=across(d), device_id_type=pl.DeviceIdType.MESH)

    direction = 1 - 2 * group
    partner = [
        lax.rem(place + direction * offset_ref[0, q] + count, count) for q in range(count)
    ]
    lane = lax.broadcasted_iota(jnp.int32, (TILE, cells), 1)

    def window(t, shift=0):
        return pl.ds(pl.multiple_of(t * TILE, TILE) + (TILE - shift), TILE)

    own_rate = scaled_rates(rates_ref, group)
    wide = jnp.full((TILE, cells), rates_ref[0, 12], jnp.float32) * 2.0
    core_wide = jnp.full((TILE, cells), rates_ref[1, 12], jnp.float32)
    ratio = jnp.where(annulus, wide, core_wide) / jnp.where(annulus, core_wide, wide)
    sign = jnp.where(annulus, -1.0, 1.0)

    def first_plane(r, outgoing):
        def body(t, carry):
            here = pl.ds(pl.multiple_of(t * TILE, TILE), TILE)
            post, (density, _, speed) = collide([source[i, r, here] for i in range(27)], own_rate)
            for i in range(27):
                first[i, r, window(t)] = post[i]
            if outgoing:
                rho = density * (1.0 / 216.0)
                base = 1.0 - 1.5 * (speed[0] * speed[0] + speed[1] * speed[1] + speed[2] * speed[2])
                radial = sign * speed[0]
                for k in range(9):
                    project = radial
                    if k // 3 != 1:
                        project = project + float(k // 3 - 1) * speed[1]
                    if k % 3 != 1:
                        project = project + float(k % 3 - 1) * speed[2]
                    balance = rho * (base + project * (3.0 + 4.5 * project))
                    value = jnp.where(annulus, post[k], post[18 + k])
                    value = balance + ratio * (value - balance)
                    if slots >= TILE:
                        part = slots // TILE
                        outward[t // part, k, pl.ds(lax.rem(t, part) * TILE, TILE)] = value
                    else:
                        for n in range(TILE // slots):
                            outward[t * (TILE // slots) + n, k] = value[n * slots : (n + 1) * slots]
            return carry

        lax.fori_loop(0, tiles, body, 0)

    def pack_rows(buffer, phase, combos):
        for c in combos:
            radial, r = COMBOS[c]
            for along in (-1, 0, 1):
                n = 3 * c + along + 1
                row_send[phase, 0, n : n + 1] = buffer[
                    velocity(radial, 1, along), r, TILE + rows - 1 : TILE + rows
                ]
                row_send[phase, 1, n : n + 1] = buffer[velocity(radial, -1, along), r, TILE : TILE + 1]

    def pack_columns(buffer, phase, combos, start):
        def body(t, carry):
            here = pl.ds(pl.multiple_of(t * TILE, TILE), TILE)
            for side, along in ((0, 1), (1, -1)):
                packed = jnp.zeros((TILE, cells), jnp.float32) if start else col_send[phase, side, here]
                for c in combos:
                    radial, r = COMBOS[c]
                    for around in (-1, 0, 1):
                        n = 3 * c + around + 1
                        value = buffer[velocity(radial, around, along), r, window(t)]
                        turn = n + 1 if along == 1 else n
                        value = value if turn == 0 else pltpu.roll(value, turn, 1)
                        packed = jnp.where(lane == n, value, packed)
                col_send[phase, side, here] = packed
            return carry

        lax.fori_loop(0, tiles, body, 0)

    def edge_copies(phase):
        top = pl.ds(0, TILE)
        inner = pl.ds(TILE, rows)
        bottom = pl.ds(rows - TILE, TILE)
        after = pl.ds(rows + TILE, TILE)
        plan = []
        for side, step in ((0, 1), (1, -1)):
            sent, landing = col_send.at[phase, side], col_recv.at[phase, side]
            plan.append((row_send.at[phase, side], row_recv.at[phase, side], (step, 0)))
            plan.append((sent, landing.at[inner], (0, step)))
            plan.append((sent.at[bottom], landing.at[top], (1, step)))
            plan.append((sent.at[top], landing.at[after], (-1, step)))
        return [
            pltpu.make_async_remote_copy(
                src_ref=src,
                dst_ref=dst,
                send_sem=edge_send_sem.at[phase, k],
                recv_sem=edge_recv_sem.at[phase, k],
                device_id=device(*step),
                device_id_type=pl.DeviceIdType.MESH,
            )
            for k, (src, dst, step) in enumerate(plan)
        ]

    def unpack_rows(buffer, phase, combos):
        for c in combos:
            radial, r = COMBOS[c]
            for along in (-1, 0, 1):
                n = 3 * c + along + 1
                buffer[velocity(radial, 1, along), r, TILE - 1 : TILE] = row_recv[phase, 0, n : n + 1]
                buffer[velocity(radial, -1, along), r, TILE + rows : TILE + rows + 1] = row_recv[
                    phase, 1, n : n + 1
                ]

    def moved(buffer, phase, radial, r, around, along, t, index):
        value = buffer[index, r, window(t, around)]
        if along == 0:
            return value
        n = 3 * COMBOS.index((radial, r)) + around + 1
        side = 0 if along == 1 else 1
        edge = col_recv[phase, side, window(t, around)]
        spot = 0 if along == 1 else cells - 1
        turn = (spot - n) % cells
        edge = edge if turn == 0 else pltpu.roll(edge, turn, 1)
        return jnp.where(lane == spot, edge, pltpu.roll(value, along % cells, 1))

    def streamed(buffer, phase, r, t, low):
        values = []
        for index in range(27):
            radial, around, along = index // 9 - 1, index // 3 % 3 - 1, index % 3 - 1
            if radial == 1 and r == 0:
                if low == "mirror":
                    value = moved(buffer, phase, -1, 0, around, along, t, index - 18)
                else:
                    value = ghost[index - 18, pl.ds(pl.multiple_of(t * TILE, TILE), TILE)]
            elif radial == -1 and r == 1:
                if low == "mirror":
                    value = ghost[index, pl.ds(pl.multiple_of(t * TILE, TILE), TILE)]
                else:
                    value = buffer[26 - index, 1, window(t)]
            else:
                value = moved(buffer, phase, radial, r - radial, around, along, t, index)
            values.append(value)
        return values

    def finish_plane(buffer, phase, r, low):
        def body(t, carry):
            here = pl.ds(pl.multiple_of(t * TILE, TILE), TILE)
            values = streamed(buffer, phase, r, t, low)
            for index in range(27):
                result[index, r, here] = values[index]
            return carry

        lax.fori_loop(0, tiles, body, 0)

    def store(r):
        return pltpu.make_async_copy(result.at[:, r], out_ref.at[0, :, r], store_sem.at[r])

    tile_copies = [
        pltpu.make_async_remote_copy(
            src_ref=tile_send.at[d],
            dst_ref=tile_recv.at[place],
            send_sem=tile_send_sem.at[d],
            recv_sem=tile_recv_sem.at[place],
            device_id=across(d),
            device_id_type=pl.DeviceIdType.MESH,
        )
        for d in range(count)
    ]

    loads[0].wait()
    first_plane(face, True)
    for d in range(count):
        chosen = jnp.int32(0)
        for q in range(1, count):
            chosen = jnp.where(partner[q] == d, q, chosen)
        tile_send[d] = outward[chosen]
        if d == 0:
            pl.semaphore_wait(barrier, len(sides) + count)
        tile_copies[d].start()

    loads[1].wait()
    first_plane(back, False)
    pack_rows(first, 0, range(5))
    pack_columns(first, 0, range(5), True)
    edges = edge_copies(0)
    for copy in edges:
        copy.start()
    for copy in edges:
        copy.wait_recv()
    unpack_rows(first, 0, range(5))

    def take_ghost():
        for s in range(count):
            pltpu.make_async_remote_copy(
                src_ref=tile_send.at[s],
                dst_ref=tile_recv.at[s],
                send_sem=tile_send_sem.at[s],
                recv_sem=tile_recv_sem.at[s],
                device_id=across(s),
                device_id_type=pl.DeviceIdType.MESH,
            ).wait_recv()
        for q in range(count):
            ghost[:, q * slots : (q + 1) * slots] = tile_recv[partner[q]]

    @pl.when(annulus)
    def _():
        def middle_plane(r):
            def body(t, carry):
                post, _ = collide(streamed(first, 0, r, t, "ghost"), own_rate)
                for i in range(27):
                    second[i, r, window(t)] = post[i]
                return carry

            lax.fori_loop(0, tiles, body, 0)

        middle_plane(1)
        pack_rows(second, 1, (2, 3))
        pack_columns(second, 1, (2, 3), True)
        take_ghost()
        middle_plane(0)
        pack_rows(second, 1, (0, 1))
        pack_columns(second, 1, (0, 1), False)
        later = edge_copies(1)
        for copy in later:
            copy.start()
        for copy in later:
            copy.wait_recv()
        unpack_rows(second, 1, range(4))
        for r in (0, 1):
            finish_plane(second, 1, r, "ghost")
            store(r).start()
        for copy in later:
            copy.wait_send()

    @pl.when(group == 1)
    def _():
        finish_plane(first, 0, 0, "mirror")
        store(0).start()
        take_ghost()
        finish_plane(first, 0, 1, "mirror")
        store(1).start()

    for copy in edges + tile_copies:
        copy.wait_send()
    for r in (0, 1):
        store(r).wait()


def local(count, length, populations, relax_rates, tile_offsets):
    _, speeds, radial, rows, cells = populations.shape
    slots = rows // count
    f32 = jnp.float32
    tall = rows + 2 * TILE
    return pl.pallas_call(
        functools.partial(kernel, count, length),
        out_shape=jax.ShapeDtypeStruct(populations.shape, f32),
        in_specs=[
            pl.BlockSpec(memory_space=pl.ANY),
            pl.BlockSpec(memory_space=pltpu.SMEM),
            pl.BlockSpec(memory_space=pltpu.SMEM),
        ],
        out_specs=pl.BlockSpec(memory_space=pl.ANY),
        scratch_shapes=[
            pltpu.VMEM((speeds, radial, rows, cells), f32),
            pltpu.VMEM((speeds, radial, tall, cells), f32),
            pltpu.VMEM((speeds, radial, tall, cells), f32),
            pltpu.VMEM((speeds, radial, rows, cells), f32),
            pltpu.VMEM((count, 9, slots, cells), f32),
            pltpu.VMEM((count, 9, slots, cells), f32),
            pltpu.VMEM((count, 9, slots, cells), f32),
            pltpu.VMEM((9, rows, cells), f32),
            pltpu.VMEM((2, 2, 16, cells), f32),
            pltpu.VMEM((2, 2, 16, cells), f32),
            pltpu.VMEM((2, 2, rows, cells), f32),
            pltpu.VMEM((2, 2, tall, cells), f32),
            pltpu.SemaphoreType.DMA((2,)),
            pltpu.SemaphoreType.DMA((2,)),
            pltpu.SemaphoreType.DMA((count,)),
            pltpu.SemaphoreType.DMA((count,)),
            pltpu.SemaphoreType.DMA((2, 8)),
            pltpu.SemaphoreType.DMA((2, 8)),
        ],
        compiler_params=pltpu.CompilerParams(
            collective_id=0, has_side_effects=True, vmem_limit_bytes=32 * 1024 * 1024
        ),
    )(populations, relax_rates, tile_offsets)


def solution(mesh):
    in_specs = (P("grp", None, None, "az", "ax"), P(), P("ax", None))
    out_specs = P("grp", None, None, "az", "ax")
    body = functools.partial(local, mesh.shape["az"], mesh.shape["ax"])
    return jax.shard_map(body, mesh=mesh, in_specs=in_specs, out_specs=out_specs, check_vma=False)
```

time: 64.7 us -> 21.8 us (0.34); the launches traced: 63.5 us -> 21.6 us
  Pallas kernels: 0 us -> 18.2 us
  matrix products: 15.9 us -> 0 us
  starting transfers between devices: 14.5 us -> 0 us
  waiting for transfers between devices: 10.2 us -> 0 us
  other arithmetic: 10.1 us -> 0 us
  local copies, waits for them, and re-layouts: 9.68 us -> 3.41 us
  between operations: 3.25 us -> 0.01 us
    pallas_call x0 -> x1, Pallas kernels: none -> 18.2 us  [local(): pl.pallas_call(functools.partial(kernel, count, length), out_shape=jax.Sh...]
    dot_general x14 -> x0, matrix products: 15.9 us -> none  [the longest x3 4.36 us: equilibrium(): jnp.einsum('ik,i...->k...', drift_table, state, precision=exact_mode)]
    ppermute x8 -> x0, waiting for transfers between devices: 10.2 us -> none  [the longest x4 10.2 us: padded_2(): before = lax.ppermute(last, axis, up)]
    ppermute x8 -> x0, starting transfers between devices: 10 us -> none  [the longest x4 7.43 us: padded_2(): after = lax.ppermute(first, axis, down)]
    all_to_all x1 -> x0, starting transfers between devices: 4.48 us -> none  [local(): lax.all_to_all(stacked, ('grp', 'az'), split_axis=0, concat_axis=0, tiled...]
    slice x16 -> x0, local copies, waits for them, and re-layouts: 3.36 us -> none  [the longest x6 1.73 us: padded_2(): last = lax.slice_in_dim(x, length - width, length, axis=dim)]
    slice x7 -> x0, other arithmetic: 3.04 us -> none  [the longest x4 1.6 us: stream(): moved = jnp.concatenate([low_ghost[index - 18][None], moved[:-1]], axis=0)]
    sub x4 -> x0, other arithmetic: 2.28 us -> none  [the longest x2 1.22 us: relax(): state - equilibrium(state)]
  transfers between devices with their start and end apart: 9 -> 0, of which waited for: 3 -> 0; matrix products, arithmetic and copies ran while one was open for 17% -> 0% of each run, Pallas kernels for 0% -> 0%
where the time goes in v1:
time: 21.8 us; the launch traced here: 21.6 us
  Pallas kernels  18.2 us (83%)
  local copies, waits for them, and re-layouts  3.41 us (16%)
    pallas_call x1, Pallas kernels, local(): pl.pallas_call(functools.partial(kernel, count, length), out_shape=jax.Sh...  18.2 us
    unnamed x7, local copies, waits for them, and re-layouts  3.41 us

profile of v1, /device:TPU:0, one launch (start us, length us, event | category | flops | bytes accessed | tf_op | source)
XLA Modules:
  0.0 21.6 jit_solution(6032550991907256023)
XLA Ops:
  0.0 0.0 copy-start
  0.0 1.2 %copy-done = f32[1,27,2,32,128]{4,3,2,1,0:T(8,128)S(1)} copy-done((f32[1,27,2,32,128]{4,3,2,1,0:T(8,128)S(1)}, f32[1,27,2,32,128]{4,3,2,1,0:T(8,128)}, u32[]{:S(2)}) %copy-start) | copy-done | bytes 884760
  1.2 0.0 copy-start.1
  1.2 0.7 %copy-done.1 = f32[2,27]{1,0:T(2,128)S(1)} copy-done((f32[2,27]{1,0:T(2,128)S(1)}, f32[2,27]{1,0:T(2,128)}, u32[]{:S(2)}) %copy-start.1) | copy-done | bytes 240
  1.8 0.0 copy-start.2
  1.9 0.7 %copy-done.2 = s32[1,4]{1,0:T(1,128)S(1)} copy-done((s32[1,4]{1,0:T(1,128)S(1)}, s32[1,4]{1,0:T(1,128)}, u32[]{:S(2)}) %copy-start.2) | copy-done | bytes 40
  2.5 18.2 %shard_map.37 = f32[1,27,2,32,128]{4,3,2,1,0:T(8,128)S(1)} custom-call(f32[1,27,2,32,128]{4,3,2,1,0:T(8,128)S(1)} %copy-done, f32[2,27]{1,0:T(2,128)S(1)} %copy-done.1, s32[1,4]{1,0:T(1,128)S(1)} %copy-done.2), custom_call_target="tpu_custom_call" | custom-call | tf_op jit(solution)/shard_map/pallas_call | solution.py:399
  20.7 0.9 %copy.5 = f32[1,27,2,32,128]{4,3,2,1,0:T(8,128)} copy(f32[1,27,2,32,128]{4,3,2,1,0:T(8,128)S(1)} %shard_map.37) | data formatting | bytes 1769472
Async XLA Ops:
  0.0 1.2 %copy-start = (f32[1,27,2,32,128]{4,3,2,1,0:T(8,128)S(1)}, f32[1,27,2,32,128]{4,3,2,1,0:T(8,128)}, u32[]{:S(2)}) copy-start(f32[1,27,2,32,128]{4,3,2,1,0:T(8,128)} %pop_ref.1) | copy-start | bytes 2654212
  1.2 0.7 %copy-start.1 = (f32[2,27]{1,0:T(2,128)S(1)}, f32[2,27]{1,0:T(2,128)}, u32[]{:S(2)}) copy-start(f32[2,27]{1,0:T(2,128)} %rates_ref.1) | copy-start | bytes 652
  1.8 0.7 %copy-start.2 = (s32[1,4]{1,0:T(1,128)S(1)}, s32[1,4]{1,0:T(1,128)}, u32[]{:S(2)}) copy-start(s32[1,4]{1,0:T(1,128)} %offset_ref.1) | copy-start | bytes 52

commit v2 on v1

--- a/solution.py
+++ b/solution.py
@@ -93,13 +93,14 @@
     count,
     length,
     pop_ref,
+    rates_hbm,
+    offset_hbm,
+    out_ref,
     rates_ref,
     offset_ref,
-    out_ref,
     source,
     first,
     second,
-    result,
     outward,
     tile_send,
     tile_recv,
@@ -109,7 +110,6 @@
     col_send,
     col_recv,
     load_sem,
-    store_sem,
     tile_send_sem,
     tile_recv_sem,
     edge_send_sem,
@@ -126,11 +126,20 @@
     face = group
     back = 1 - group
 
-    loads = [
-        pltpu.make_async_copy(pop_ref.at[0, :, r], source.at[:, r], load_sem.at[k])
-        for k, r in enumerate((face, back))
+    settings = [
+        pltpu.make_async_copy(rates_hbm, rates_ref, load_sem.at[tiles + 1]),
+        pltpu.make_async_copy(offset_hbm, offset_ref, load_sem.at[tiles + 2]),
     ]
-    for copy in loads:
+    loads = []
+    for t in range(tiles):
+        here = pl.ds(t * TILE, TILE)
+        loads.append(
+            pltpu.make_async_copy(
+                pop_ref.at[0, :, face, here], source.at[:, face, here], load_sem.at[t]
+            )
+        )
+    rest = pltpu.make_async_copy(pop_ref.at[0, :, back], source.at[:, back], load_sem.at[tiles])
+    for copy in settings + loads + [rest]:
         copy.start()
 
     def device(around, along):
@@ -150,6 +159,8 @@
     for d in range(count):
         pl.semaphore_signal(barrier, 1, device_id=across(d), device_id_type=pl.DeviceIdType.MESH)
 
+    for copy in settings:
+        copy.wait()
     direction = 1 - 2 * group
     partner = [
         lax.rem(place + direction * offset_ref[0, q] + count, count) for q in range(count)
@@ -168,6 +179,10 @@
     def first_plane(r, outgoing):
         def body(t, carry):
             here = pl.ds(pl.multiple_of(t * TILE, TILE), TILE)
+            if outgoing:
+                pltpu.make_async_copy(
+                    pop_ref.at[0, :, r, here], source.at[:, r, here], load_sem.at[t]
+                ).wait()
             post, (density, _, speed) = collide([source[i, r, here] for i in range(27)], own_rate)
             for i in range(27):
                 first[i, r, window(t)] = post[i]
@@ -292,13 +307,10 @@
             here = pl.ds(pl.multiple_of(t * TILE, TILE), TILE)
             values = streamed(buffer, phase, r, t, low)
             for index in range(27):
-                result[index, r, here] = values[index]
+                out_ref[0, index, r, here] = values[index]
             return carry
 
         lax.fori_loop(0, tiles, body, 0)
-
-    def store(r):
-        return pltpu.make_async_copy(result.at[:, r], out_ref.at[0, :, r], store_sem.at[r])
 
     tile_copies = [
         pltpu.make_async_remote_copy(
@@ -312,7 +324,6 @@
         for d in range(count)
     ]
 
-    loads[0].wait()
     first_plane(face, True)
     for d in range(count):
         chosen = jnp.int32(0)
@@ -323,7 +334,7 @@
             pl.semaphore_wait(barrier, len(sides) + count)
         tile_copies[d].start()
 
-    loads[1].wait()
+    rest.wait()
     first_plane(back, False)
     pack_rows(first, 0, range(5))
     pack_columns(first, 0, range(5), True)
@@ -373,22 +384,17 @@
         unpack_rows(second, 1, range(4))
         for r in (0, 1):
             finish_plane(second, 1, r, "ghost")
-            store(r).start()
         for copy in later:
             copy.wait_send()
 
     @pl.when(group == 1)
     def _():
         finish_plane(first, 0, 0, "mirror")
-        store(0).start()
         take_ghost()
         finish_plane(first, 0, 1, "mirror")
-        store(1).start()
 
     for copy in edges + tile_copies:
         copy.wait_send()
-    for r in (0, 1):
-        store(r).wait()
 
 
 def local(count, length, populations, relax_rates, tile_offsets):
@@ -400,16 +406,17 @@
         functools.partial(kernel, count, length),
         out_shape=jax.ShapeDtypeStruct(populations.shape, f32),
         in_specs=[
-            pl.BlockSpec(memory_space=pl.ANY),
-            pl.BlockSpec(memory_space=pltpu.SMEM),
-            pl.BlockSpec(memory_space=pltpu.SMEM),
+            pl.BlockSpec(memory_space=pltpu.HBM),
+            pl.BlockSpec(memory_space=pltpu.HBM),
+            pl.BlockSpec(memory_space=pltpu.HBM),
         ],
-        out_specs=pl.BlockSpec(memory_space=pl.ANY),
+        out_specs=pl.BlockSpec(memory_space=pltpu.VMEM),
         scratch_shapes=[
+            pltpu.SMEM(relax_rates.shape, f32),
+            pltpu.SMEM(tile_offsets.shape, jnp.int32),
             pltpu.VMEM((speeds, radial, rows, cells), f32),
             pltpu.VMEM((speeds, radial, tall, cells), f32),
             pltpu.VMEM((speeds, radial, tall, cells), f32),
-            pltpu.VMEM((speeds, radial, rows, cells), f32),
             pltpu.VMEM((count, 9, slots, cells), f32),
             pltpu.VMEM((count, 9, slots, cells), f32),
             pltpu.VMEM((count, 9, slots, cells), f32),
@@ -418,8 +425,7 @@
             pltpu.VMEM((2, 2, 16, cells), f32),
             pltpu.VMEM((2, 2, rows, cells), f32),
             pltpu.VMEM((2, 2, tall, cells), f32),
-            pltpu.SemaphoreType.DMA((2,)),
-            pltpu.SemaphoreType.DMA((2,)),
+            pltpu.SemaphoreType.DMA((rows // TILE + 3,)),
             pltpu.SemaphoreType.DMA((count,)),
             pltpu.SemaphoreType.DMA((count,)),
             pltpu.SemaphoreType.DMA((2, 8)),
@@ -428,7 +434,7 @@
         compiler_params=pltpu.CompilerParams(
             collective_id=0, has_side_effects=True, vmem_limit_bytes=32 * 1024 * 1024
         ),
-    )(populations, relax_rates, tile_offsets)
+    )(*(pltpu.with_memory_space_constraint(x, pltpu.HBM) for x in (populations, relax_rates, tile_offsets)))
 
 
 def solution(mesh):

time: 21.8 us -> 18.5 us (0.85)
  local copies, waits for them, and re-layouts: 3.41 us -> 0.91 us
  Pallas kernels: 18.2 us -> 17.5 us
    unnamed x7 -> x1, local copies, waits for them, and re-layouts: 3.41 us -> 0.91 us
    pallas_call x1, Pallas kernels: 18.2 us -> 17.5 us  [local(): pl.pallas_call(functools.partial(kernel, count, length), out_shape=jax.Sh...]
where the time goes in v2:
time: 18.5 us; the launch traced here: 18.4 us
  Pallas kernels  17.5 us (95%)
  local copies, waits for them, and re-layouts  0.91 us (5%)
    pallas_call x1, Pallas kernels, local(): pl.pallas_call(functools.partial(kernel, count, length), out_shape=jax.Sh...  17.5 us
    unnamed x1, local copies, waits for them, and re-layouts  0.91 us

profile of v2, /device:TPU:0, one launch (start us, length us, event | category | flops | bytes accessed | tf_op | source)
XLA Modules:
  0.0 18.4 jit_solution(7342048623364377812)
XLA Ops:
  0.0 17.5 %shard_map.37 = f32[1,27,2,32,128]{4,3,2,1,0:T(8,128)S(1)} custom-call(f32[1,27,2,32,128]{4,3,2,1,0:T(8,128)} %pop_ref.1, f32[2,27]{1,0:T(2,128)} %rates_hbm.1, s32[1,4]{1,0:T(1,128)} %offset_hbm.1), custom_call_target="tpu_custom_call" | custom-call | tf_op jit(solution)/shard_map/pallas_call | solution.py:405
  17.5 0.9 %copy.5 = f32[1,27,2,32,128]{4,3,2,1,0:T(8,128)} copy(f32[1,27,2,32,128]{4,3,2,1,0:T(8,128)S(1)} %shard_map.37) | data formatting | bytes 1769472

commit v3 on v2

--- a/solution.py
+++ b/solution.py
@@ -89,26 +89,103 @@
     return out
 
 
+def streamer(ghost, col_recv):
+    cells = ghost.shape[2]
+    lane = lax.broadcasted_iota(jnp.int32, (TILE, cells), 1)
+
+    def window(t, shift=0):
+        return pl.ds(pl.multiple_of(t * TILE, TILE) + (TILE - shift), TILE)
+
+    def moved(buffer, phase, radial, r, around, along, t, index):
+        value = buffer[index, r, window(t, around)]
+        if along == 0:
+            return value
+        n = 3 * COMBOS.index((radial, r)) + around + 1
+        side = 0 if along == 1 else 1
+        edge = col_recv[phase, side, window(t, around)]
+        spot = 0 if along == 1 else cells - 1
+        turn = (spot - n) % cells
+        edge = edge if turn == 0 else pltpu.roll(edge, turn, 1)
+        return jnp.where(lane == spot, edge, pltpu.roll(value, along % cells, 1))
+
+    def streamed(buffer, phase, r, t, low):
+        values = []
+        for index in range(27):
+            radial, around, along = index // 9 - 1, index // 3 % 3 - 1, index % 3 - 1
+            if radial == 1 and r == 0:
+                if low == "mirror":
+                    value = moved(buffer, phase, -1, 0, around, along, t, index - 18)
+                else:
+                    value = ghost[index - 18, pl.ds(pl.multiple_of(t * TILE, TILE), TILE)]
+            elif radial == -1 and r == 1:
+                if low == "mirror":
+                    value = ghost[index, pl.ds(pl.multiple_of(t * TILE, TILE), TILE)]
+                else:
+                    value = buffer[26 - index, 1, window(t)]
+            else:
+                value = moved(buffer, phase, radial, r - radial, around, along, t, index)
+            values.append(value)
+        return values
+
+    return streamed
+
+
+def final_kernel(first, second, ghost, col_recv, out_ref, result, store_sem):
+    tiles = ghost.shape[1] // TILE
+    streamed = streamer(ghost, col_recv)
+    group = lax.axis_index("grp")
+
+    def store(r, t):
+        here = pl.ds(pl.multiple_of(t * TILE, TILE), TILE)
+        return pltpu.make_async_copy(
+            result.at[:, r, here], out_ref.at[0, :, r, here], store_sem.at[r, t]
+        )
+
+    def finish_planes(buffer, phase, low):
+        for r in (0, 1):
+
+            def body(t, carry):
+                here = pl.ds(pl.multiple_of(t * TILE, TILE), TILE)
+                values = streamed(buffer, phase, r, t, low)
+                for index in range(27):
+                    result[index, r, here] = values[index]
+                store(r, t).start()
+                return carry
+
+            lax.fori_loop(0, tiles, body, 0)
+
+    @pl.when(group == 0)
+    def _():
+        finish_planes(second, 1, "ghost")
+
+    @pl.when(group == 1)
+    def _():
+        finish_planes(first, 0, "mirror")
+
+    for r in (0, 1):
+        for t in range(tiles):
+            store(r, t).wait()
+
+
 def kernel(
     count,
     length,
     pop_ref,
     rates_hbm,
     offset_hbm,
-    out_ref,
+    first,
+    second,
+    ghost,
+    col_recv,
     rates_ref,
     offset_ref,
     source,
-    first,
-    second,
     outward,
     tile_send,
     tile_recv,
-    ghost,
     row_send,
     row_recv,
     col_send,
-    col_recv,
     load_sem,
     tile_send_sem,
     tile_recv_sem,
@@ -142,12 +219,16 @@
     for copy in settings + loads + [rest]:
         copy.start()
 
+    def wrapped(value, size):
+        value = jnp.where(value < 0, value + size, value)
+        return jnp.where(value >= size, value - size, value)
+
+    near_az = {i: wrapped(place + i, count) if i else place for i in (-1, 0, 1)}
+    near_ax = {j: wrapped(block + j, length) if j else block for j in (-1, 0, 1)}
+    spread = [wrapped(place + i, count) if i else place for i in range(count)]
+
     def device(around, along):
-        return {
-            "grp": group,
-            "az": lax.rem(place + around + count, count),
-            "ax": lax.rem(block + along + length, length),
-        }
+        return {"grp": group, "az": near_az[around], "ax": near_ax[along]}
 
     def across(position):
         return {"grp": 1 - group, "az": position, "ax": block}
@@ -162,9 +243,7 @@
     for copy in settings:
         copy.wait()
     direction = 1 - 2 * group
-    partner = [
-        lax.rem(place + direction * offset_ref[0, q] + count, count) for q in range(count)
-    ]
+    partner = [wrapped(place + direction * offset_ref[0, q], count) for q in range(count)]
     lane = lax.broadcasted_iota(jnp.int32, (TILE, cells), 1)
 
     def window(t, shift=0):
@@ -271,46 +350,7 @@
                     phase, 1, n : n + 1
                 ]
 
-    def moved(buffer, phase, radial, r, around, along, t, index):
-        value = buffer[index, r, window(t, around)]
-        if along == 0:
-            return value
-        n = 3 * COMBOS.index((radial, r)) + around + 1
-        side = 0 if along == 1 else 1
-        edge = col_recv[phase, side, window(t, around)]
-        spot = 0 if along == 1 else cells - 1
-        turn = (spot - n) % cells
-        edge = edge if turn == 0 else pltpu.roll(edge, turn, 1)
-        return jnp.where(lane == spot, edge, pltpu.roll(value, along % cells, 1))
-
-    def streamed(buffer, phase, r, t, low):
-        values = []
-        for index in range(27):
-            radial, around, along = index // 9 - 1, index // 3 % 3 - 1, index % 3 - 1
-            if radial == 1 and r == 0:
-                if low == "mirror":
-                    value = moved(buffer, phase, -1, 0, around, along, t, index - 18)
-                else:
-                    value = ghost[index - 18, pl.ds(pl.multiple_of(t * TILE, TILE), TILE)]
-            elif radial == -1 and r == 1:
-                if low == "mirror":
-                    value = ghost[index, pl.ds(pl.multiple_of(t * TILE, TILE), TILE)]
-                else:
-                    value = buffer[26 - index, 1, window(t)]
-            else:
-                value = moved(buffer, phase, radial, r - radial, around, along, t, index)
-            values.append(value)
-        return values
-
-    def finish_plane(buffer, phase, r, low):
-        def body(t, carry):
-            here = pl.ds(pl.multiple_of(t * TILE, TILE), TILE)
-            values = streamed(buffer, phase, r, t, low)
-            for index in range(27):
-                out_ref[0, index, r, here] = values[index]
-            return carry
-
-        lax.fori_loop(0, tiles, body, 0)
+    streamed = streamer(ghost, col_recv)
 
     tile_copies = [
         pltpu.make_async_remote_copy(
@@ -318,7 +358,7 @@
             dst_ref=tile_recv.at[place],
             send_sem=tile_send_sem.at[d],
             recv_sem=tile_recv_sem.at[place],
-            device_id=across(d),
+            device_id=across(spread[d]),
             device_id_type=pl.DeviceIdType.MESH,
         )
         for d in range(count)
@@ -328,7 +368,7 @@
     for d in range(count):
         chosen = jnp.int32(0)
         for q in range(1, count):
-            chosen = jnp.where(partner[q] == d, q, chosen)
+            chosen = jnp.where(partner[q] == spread[d], q, chosen)
         tile_send[d] = outward[chosen]
         if d == 0:
             pl.semaphore_wait(barrier, len(sides) + count)
@@ -382,16 +422,12 @@
         for copy in later:
             copy.wait_recv()
         unpack_rows(second, 1, range(4))
-        for r in (0, 1):
-            finish_plane(second, 1, r, "ghost")
         for copy in later:
             copy.wait_send()
 
     @pl.when(group == 1)
     def _():
-        finish_plane(first, 0, 0, "mirror")
         take_ghost()
-        finish_plane(first, 0, 1, "mirror")
 
     for copy in edges + tile_copies:
         copy.wait_send()
@@ -402,29 +438,32 @@
     slots = rows // count
     f32 = jnp.float32
     tall = rows + 2 * TILE
-    return pl.pallas_call(
+    vmem = pl.BlockSpec(memory_space=pltpu.VMEM)
+    hbm = pl.BlockSpec(memory_space=pltpu.HBM)
+    inputs = [
+        pltpu.with_memory_space_constraint(x, pltpu.HBM)
+        for x in (populations, relax_rates, tile_offsets)
+    ]
+    parts = pl.pallas_call(
         functools.partial(kernel, count, length),
-        out_shape=jax.ShapeDtypeStruct(populations.shape, f32),
-        in_specs=[
-            pl.BlockSpec(memory_space=pltpu.HBM),
-            pl.BlockSpec(memory_space=pltpu.HBM),
-            pl.BlockSpec(memory_space=pltpu.HBM),
+        out_shape=[
+            jax.ShapeDtypeStruct((speeds, radial, tall, cells), f32),
+            jax.ShapeDtypeStruct((speeds, radial, tall, cells), f32),
+            jax.ShapeDtypeStruct((9, rows, cells), f32),
+            jax.ShapeDtypeStruct((2, 2, tall, cells), f32),
         ],
-        out_specs=pl.BlockSpec(memory_space=pltpu.VMEM),
+        in_specs=[hbm] * 3,
+        out_specs=[vmem] * 4,
         scratch_shapes=[
             pltpu.SMEM(relax_rates.shape, f32),
             pltpu.SMEM(tile_offsets.shape, jnp.int32),
             pltpu.VMEM((speeds, radial, rows, cells), f32),
-            pltpu.VMEM((speeds, radial, tall, cells), f32),
-            pltpu.VMEM((speeds, radial, tall, cells), f32),
             pltpu.VMEM((count, 9, slots, cells), f32),
             pltpu.VMEM((count, 9, slots, cells), f32),
             pltpu.VMEM((count, 9, slots, cells), f32),
-            pltpu.VMEM((9, rows, cells), f32),
             pltpu.VMEM((2, 2, 16, cells), f32),
             pltpu.VMEM((2, 2, 16, cells), f32),
             pltpu.VMEM((2, 2, rows, cells), f32),
-            pltpu.VMEM((2, 2, tall, cells), f32),
             pltpu.SemaphoreType.DMA((rows // TILE + 3,)),
             pltpu.SemaphoreType.DMA((count,)),
             pltpu.SemaphoreType.DMA((count,)),
@@ -432,9 +471,20 @@
             pltpu.SemaphoreType.DMA((2, 8)),
         ],
         compiler_params=pltpu.CompilerParams(
-            collective_id=0, has_side_effects=True, vmem_limit_bytes=32 * 1024 * 1024
+            collective_id=0, has_side_effects=True, vmem_limit_bytes=12 * 1024 * 1024
         ),
-    )(*(pltpu.with_memory_space_constraint(x, pltpu.HBM) for x in (populations, relax_rates, tile_offsets)))
+    )(*inputs)
+    return pl.pallas_call(
+        final_kernel,
+        out_shape=jax.ShapeDtypeStruct(populations.shape, f32),
+        in_specs=[vmem] * 4,
+        out_specs=hbm,
+        scratch_shapes=[
+            pltpu.VMEM((speeds, radial, rows, cells), f32),
+            pltpu.SemaphoreType.DMA((radial, rows // TILE)),
+        ],
+        compiler_params=pltpu.CompilerParams(vmem_limit_bytes=16 * 1024 * 1024),
+    )(*parts)
 
 
 def solution(mesh):

time: 18.5 us -> 18.4 us (level)
  local copies, waits for them, and re-layouts: 0.91 us -> 0 us
  Pallas kernels: 17.5 us -> 18.2 us
    unnamed x1 -> x0, local copies, waits for them, and re-layouts: 0.91 us -> none
    pallas_call x1 -> x2, Pallas kernels: 17.5 us -> 18.2 us  [the longest x1 16.7 us: local(): pl.pallas_call(functools.partial(kernel, count, length), out_shape=[jax.S...]
where the time goes in v3:
time: 18.4 us; the launch traced here: 18.2 us
  Pallas kernels  18.2 us (99%)
    pallas_call x1, Pallas kernels, local(): pl.pallas_call(functools.partial(kernel, count, length), out_shape=[jax.S...  16.7 us
    pallas_call x1, Pallas kernels, local(): pl.pallas_call(final_kernel, out_shape=jax.ShapeDtypeStruct(populations.s...  1.52 us

profile of v3, /device:TPU:0, one launch (start us, length us, event | category | flops | bytes accessed | tf_op | source)
XLA Modules:
  0.0 18.2 jit_solution(17146014627585435998)
XLA Ops:
  0.0 16.7 %shard_map.37 = (f32[27,2,48,128]{3,2,1,0:T(8,128)S(1)}, f32[27,2,48,128]{3,2,1,0:T(8,128)S(1)}, f32[9,32,128]{2,1,0:T(8,128)S(1)}, f32[2,2,48,128]{3,2,1,0:T(8,128)S(1)}) custom-call(f32[1,27,2,32,128]{4,3,2,1,0:T(8,128)} %pop_ref.1, f32[2,27]{1,0:T(2,128)} %rates_hbm.1, s32[1,4]{1,0:T(1,128)} %offset_hbm.1), custom_call_target="tpu_custom_call" | custom-call | tf_op jit(solution)/shard_map/pallas_call | solution.py:447
  16.7 1.5 %shard_map.38 = f32[1,27,2,32,128]{4,3,2,1,0:T(8,128)} custom-call(f32[27,2,48,128]{3,2,1,0:T(8,128)S(1)} %get-tuple-element.9.first, f32[27,2,48,128]{3,2,1,0:T(8,128)S(1)} %get-tuple-element.10.second, f32[9,32,128]{2,1,0:T(8,128)S(1)} %get-tuple-element.11.ghost, f32[2,2,48,128]{3,2,1,0:T(8,128)S(1)} %get-tuple-element.12.col_recv), custom_call_target="tpu_custom_call" | custom-call | tf_op jit(solution)/shard_map/pallas_call | solution.py:477

commit v4 on v3

--- a/solution.py
+++ b/solution.py
@@ -152,7 +152,7 @@
                 store(r, t).start()
                 return carry
 
-            lax.fori_loop(0, tiles, body, 0)
+            lax.fori_loop(0, tiles, body, 0, unroll=True)
 
     @pl.when(group == 0)
     def _():
@@ -286,7 +286,7 @@
                             outward[t * (TILE // slots) + n, k] = value[n * slots : (n + 1) * slots]
             return carry
 
-        lax.fori_loop(0, tiles, body, 0)
+        lax.fori_loop(0, tiles, body, 0, unroll=True)
 
     def pack_rows(buffer, phase, combos):
         for c in combos:
@@ -314,7 +314,7 @@
                 col_send[phase, side, here] = packed
             return carry
 
-        lax.fori_loop(0, tiles, body, 0)
+        lax.fori_loop(0, tiles, body, 0, unroll=True)
 
     def edge_copies(phase):
         top = pl.ds(0, TILE)
@@ -407,7 +407,7 @@
                     second[i, r, window(t)] = post[i]
                 return carry
 
-            lax.fori_loop(0, tiles, body, 0)
+            lax.fori_loop(0, tiles, body, 0, unroll=True)
 
         middle_plane(1)
         pack_rows(second, 1, (2, 3))

time: 18.4 us -> 16.7 us (0.908)
  Pallas kernels: 18.2 us -> 16.6 us
    pallas_call x1, Pallas kernels: 16.7 us -> 15.5 us  [local(): pl.pallas_call(functools.partial(kernel, count, length), out_shape=[jax.S...]
    pallas_call x1, Pallas kernels: 1.52 us -> 1.08 us  [local(): pl.pallas_call(final_kernel, out_shape=jax.ShapeDtypeStruct(populations.s...]
where the time goes in v4:
time: 16.7 us; the launch traced here: 16.6 us
  Pallas kernels  16.6 us (99%)
    pallas_call x1, Pallas kernels, local(): pl.pallas_call(functools.partial(kernel, count, length), out_shape=[jax.S...  15.5 us
    pallas_call x1, Pallas kernels, local(): pl.pallas_call(final_kernel, out_shape=jax.ShapeDtypeStruct(populations.s...  1.08 us

profile of v4, /device:TPU:0, one launch (start us, length us, event | category | flops | bytes accessed | tf_op | source)
XLA Modules:
  0.0 16.6 jit_solution(2490437815285481020)
XLA Ops:
  0.0 15.5 %shard_map.37 = (f32[27,2,48,128]{3,2,1,0:T(8,128)S(1)}, f32[27,2,48,128]{3,2,1,0:T(8,128)S(1)}, f32[9,32,128]{2,1,0:T(8,128)S(1)}, f32[2,2,48,128]{3,2,1,0:T(8,128)S(1)}) custom-call(f32[1,27,2,32,128]{4,3,2,1,0:T(8,128)} %pop_ref.1, f32[2,27]{1,0:T(2,128)} %rates_hbm.1, s32[1,4]{1,0:T(1,128)} %offset_hbm.1), custom_call_target="tpu_custom_call" | custom-call | tf_op jit(solution)/shard_map/pallas_call | solution.py:447
  15.5 1.1 %shard_map.38 = f32[1,27,2,32,128]{4,3,2,1,0:T(8,128)} custom-call(f32[27,2,48,128]{3,2,1,0:T(8,128)S(1)} %get-tuple-element.9.first, f32[27,2,48,128]{3,2,1,0:T(8,128)S(1)} %get-tuple-element.10.second, f32[9,32,128]{2,1,0:T(8,128)S(1)} %get-tuple-element.11.ghost, f32[2,2,48,128]{3,2,1,0:T(8,128)S(1)} %get-tuple-element.12.col_recv), custom_call_target="tpu_custom_call" | custom-call | tf_op jit(solution)/shard_map/pallas_call | solution.py:477
